TPU v7x, 32 devices: a whole 2x2x4 slice. The times are simulated.
32 devices in a mesh: dp: 4 (over x, core), depth: 2 (over y), height: 4 (over z).
Axes of the slice: x: 2, y: 2, z: 4, core: 2. Of those that a mesh axis runs over, the one named last changes fastest.
Arguments:
- act_one: bfloat16 [4, 32, 8, 64, 128], P('dp', None, 'depth', 'height'), may hold values from -6 to 6
- pre_two: bfloat16 [4, 64, 8, 64, 128], P('dp', None, 'depth', 'height'), may hold values from -6 to 6
- cot_three: bfloat16 [4, 128, 4, 2048], P('dp', None, 'depth', 'height'), may hold values from -24 to 24
- weight_two: float32 [64, 864], replicated, may hold values from -6 to 6
- weight_three: float32 [128, 1728], replicated, may hold values from -6 to 6
- moment_two: float32 [55296], P(('dp', 'depth', 'height')), may hold values from -1.2 to 1.2
- moment_three: float32 [221184], P(('dp', 'depth', 'height')), may hold values from -1.2 to 1.2
Outputs:
- grad_input: bfloat16 [4, 32, 8, 64, 128], P('dp', None, 'depth', 'height')
- new_weight_two: float32 [64, 864], replicated
- new_weight_three: float32 [128, 1728], replicated
- new_moment_two: float32 [55296], P(('dp', 'depth', 'height'))
- new_moment_three: float32 [221184], P(('dp', 'depth', 'height'))
All inputs are finite; a program needn't handle non-finite values.
Results may differ from a plain program's by a relative error of at most 0.007.
Values may be sent and summed in bfloat16 or wider, within the bound.
A program may use at most 128 MiB of HBM per device.

v0:
```python
import jax
import jax.numpy as jnp
from jax import lax
from jax.sharding import PartitionSpec as P

SLOPE = 0.3
LEARN = 4.0
TRUST = 0.05
MOMENTUM = 0.9
EPSILON = 1e-06


def padded_2(x, sides, width):
    for axis, dim in sides:
        devices, length = (lax.axis_size(axis), x.shape[dim])
        up = [(i, (i + 1) % devices) for i in range(devices - 1)]
        down = [(j, i) for i, j in up]
        last = lax.slice_in_dim(x, length - width, length, axis=dim)
        initial = lax.slice_in_dim(x, 0, width, axis=dim)
        before = lax.ppermute(last, axis, up)
        after = lax.ppermute(initial, axis, down)
        x = jnp.concatenate([before, x, after], axis=dim)
    return x


def leaky(value):
    return jnp.where(value > 0, value, SLOPE * value)


def slope_of(value):
    return jnp.where(value > 0, 1.0, SLOPE).astype(jnp.float32)


def local(act_one, pre_two, cot_three, weight_two, weight_three, moment_two, moment_three):
    chan_one = act_one.shape[1]
    chan_two = pre_two.shape[1]
    chan_three = cot_three.shape[1]
    local_d, local_h, local_w = (pre_two.shape[2], pre_two.shape[3], pre_two.shape[4])
    half_d, half_h, half_w = (local_d // 2, local_h // 2, local_w // 2)
    flat_len = half_h * half_w
    volumes = lax.axis_size("dp")
    scale_two = (chan_one * 27) ** (-0.5)
    scale_three = (chan_two * 27) ** (-0.5)
    pre_f = pre_two[0].astype(jnp.float32)
    pooled = leaky(pre_f).reshape(chan_two, half_d, 2, half_h, 2, half_w, 2).mean(axis=(2, 4, 6))
    pooled = pooled.astype(jnp.bfloat16).reshape(chan_two, half_d, flat_len)
    wb_three = weight_three.astype(jnp.bfloat16).reshape(chan_three, chan_two, 27)
    wb_two = weight_two.astype(jnp.bfloat16).reshape(chan_two, chan_one, 27)
    rim_depth = padded_2(cot_three, (("depth", 2),), 1)
    rim_both = padded_2(rim_depth, (("height", 3),), half_w)
    flat = jnp.pad(rim_both[0], ((0, 0), (0, 0), (1, 1)))
    column = lax.broadcasted_iota(jnp.int32, (1, 1, flat_len), 2) % half_w
    back = jnp.zeros((chan_two, half_d, flat_len), jnp.float32)
    grads_three = []
    for k in range(27):
        kd, kh, kw = (k // 9, k // 3 % 3, k % 3)
        od, oh, ow = (2 - kd, 2 - kh, 2 - kw)
        begin = oh * half_w + ow
        piece = flat[:, od : od + half_d, begin : begin + flat_len]
        inside = (column + ow - 1 >= 0) & (column + ow - 1 < half_w)
        piece = jnp.where(inside, piece, jnp.zeros_like(piece))
        back = back + jnp.einsum(
            "oi,odn->idn", wb_three[:, :, k], piece, preferred_element_type=jnp.float32
        )
        grads_three.append(
            jnp.einsum("odn,idn->oi", piece, pooled, preferred_element_type=jnp.float32)
        )
    back = (scale_three * back).astype(jnp.bfloat16).astype(jnp.float32)
    upper = jnp.broadcast_to(
        back.reshape(chan_two, half_d, 1, half_h, 1, half_w, 1),
        (chan_two, half_d, 2, half_h, 2, half_w, 2),
    )
    upper = upper.reshape(chan_two, local_d, local_h, local_w)
    cot_two = (upper * 0.125 * slope_of(pre_f)).astype(jnp.bfloat16)
    grads_two = []
    rim_fine = padded_2(cot_two[None], (("depth", 2), ("height", 3)), 1)[0]
    padded = jnp.pad(rim_fine, ((0, 0), (0, 0), (0, 0), (1, 1)))
    act_local = act_one[0]
    into = jnp.zeros((chan_one, local_d, local_h, local_w), jnp.float32)
    for k in range(27):
        kd, kh, kw = (k // 9, k // 3 % 3, k % 3)
        od, oh, ow = (2 - kd, 2 - kh, 2 - kw)
        piece = padded[:, od : od + local_d, oh : oh + local_h, ow : ow + local_w]
        into = into + jnp.einsum(
            "oi,odhw->idhw", wb_two[:, :, k], piece, preferred_element_type=jnp.float32
        )
        grads_two.append(
            jnp.einsum("odhw,idhw->oi", piece, act_local, preferred_element_type=jnp.float32)
        )
    grad_input = (scale_two * into).astype(jnp.bfloat16)[None]
    part_two = jnp.stack(grads_two, -1).reshape(chan_two, chan_one * 27)
    part_three = jnp.stack(grads_three, -1).reshape(chan_three, chan_two * 27)
    shard_two = moment_two.shape[0]
    shard_three = moment_three.shape[0]
    norm_w_two = jnp.sqrt(jnp.sum(weight_two * weight_two))
    norm_w_three = jnp.sqrt(jnp.sum(weight_three * weight_three))
    position = lax.axis_index(("dp", "depth", "height"))
    total_two, total_three = lax.psum((part_two, part_three), ("dp", "depth", "height"))
    grad_two = (total_two * (scale_two / volumes)).reshape(-1)
    grad_three = (total_three * (scale_three / volumes)).reshape(-1)
    trust_two = TRUST * norm_w_two / (jnp.sqrt(jnp.sum(grad_two * grad_two)) + EPSILON)
    trust_three = TRUST * norm_w_three / (jnp.sqrt(jnp.sum(grad_three * grad_three)) + EPSILON)
    own_two = lax.dynamic_slice_in_dim(grad_two, position * shard_two, shard_two)
    own_three = lax.dynamic_slice_in_dim(grad_three, position * shard_three, shard_three)
    new_moment_two = MOMENTUM * moment_two + LEARN * trust_two * own_two
    new_moment_three = MOMENTUM * moment_three + LEARN * trust_three * own_three
    full_two, full_three = (
        lax.all_gather(new_moment_two, ("dp", "depth", "height"), axis=0, tiled=True),
        lax.all_gather(new_moment_three, ("dp", "depth", "height"), axis=0, tiled=True),
    )
    new_weight_two = weight_two - full_two.reshape(weight_two.shape)
    new_weight_three = weight_three - full_three.reshape(weight_three.shape)
    return (grad_input, new_weight_two, new_weight_three, new_moment_two, new_moment_three)


def solution(mesh):
    in_specs = (
        P("dp", None, "depth", "height", None),
        P("dp", None, "depth", "height", None),
        P("dp", None, "depth", "height"),
        P(),
        P(),
        P(("dp", "depth", "height")),
        P(("dp", "depth", "height")),
    )
    out_specs = (
        P("dp", None, "depth", "height", None),
        P(),
        P(),
        P(("dp", "depth", "height")),
        P(("dp", "depth", "height")),
    )
    return jax.shard_map(local, mesh=mesh, in_specs=in_specs, out_specs=out_specs, check_vma=False)
```

profile of v0, /device:TPU:0, one launch (start us, length us, event | category | flops | bytes accessed | tf_op | source)
XLA Modules:
  0.0 565.7 jit_solution(8864990232708285337)
XLA Ops:
  7.2 2.3 fusion.267
  10.8 5.0 collective-permute-start
  15.9 2.3 multiply_reduce_fusion.1
  23.0 2.8 copy.503
  25.7 6.3 %fusion = f32[64,2,8,64]{0,3,2,1:T(8,128)S(1)} fusion(f32[64,2,2,8,2,64,2]{0,6,5,4,3,2,1:T(2,128)} %bitcast.664), kind=kLoop, calls=%fused_computation.19 | loop fusion | flops 2031616 | bytes 2359296 | tf_op jit(solution)/shard_map/reduce_sum | solution.py:45
  34.7 5.2 collective-permute-start.2
  42.5 2.3 maximum_bitcast_fusion.1
  44.8 4.7 broadcast_select_fusion.18
  49.6 4.3 broadcast_select_fusion
  54.0 3.5 broadcast_select_fusion.9
  63.5 4.0 broadcast_in_dim.160
  67.6 2.8 copy.445
  74.1 4.6 collective-permute-start.4
  86.6 5.2 collective-permute-start.6
  111.5 2.7 copy.558
  114.2 2.2 reshape.108
  116.4 122.2 %all-reduce.7.cloned.1.call-done = f32[64,864]{0,1:T(8,128)} async-done(((f32[64,864]{0,1:T(8,128)}), f32[64,864]{0,1:T(8,128)}) %all-reduce.7.cloned.1.call-update) | async-done | bytes 221200 | tf_op jit(solution)/shard_map/psum | solution.py:98
  245.0 131.8 %all-reduce.9.cloned.1.call-done = (f32[55296]{0:T(1024)}, f32[128,1728]{0,1:T(8,128)}) async-done(((f32[55296]{0:T(1024)}, f32[128,1728]{0,1:T(8,128)}), (f32[55296]{0:T(1024)}, f32[128,1728]{0,1:T(8,128)})) %all-reduce.9.cloned.1.call-update) | async-done | bytes 1105936
  380.0 5.1 fusion.263
  385.2 3.0 fusion.264
  457.2 10.9 %fusion.69 = bf16[1,32,4,16,128]{4,1,3,2,0:T(8,128)(2,1)S(1)} fusion(f32[32,4,16,128]{3,0,2,1:T(8,128)} %convolution_bitcast_fusion.1, f32[32,4,16,128]{3,0,2,1:T(8,128)} %convolution_bitcast_fusion.2, f32[32,4,16,128]{3,0,2,1:T(8,128)} %convolution_bitcast_fusion.3, f32[32,4,16,128]{3,0,2,1:T(8,128)} %convolution_bitcast_fusion.4, ...), kind=kOutput, calls=%fused_computation.213 | convolution fusion | flops 40894464 | bytes 29560832 | tf_op jit(solution)/shard_map/oi,odhw->idhw/dot_general | solution.py:84
  475.3 75.0 %all-gather = f32[32,1,6912]{2,1,0:T(1,128)S(1)} all-gather(f32[1,1,6912]{2,1,0:T(1,128)S(1)} %reshape.114), channel_id=1, replica_groups=mesh['dp'=4,'depth'=2,'height'=4] {'dp','depth','height'}, dimensions={0}, use_global_device_ids=true | all-gather | bytes 912384 | tf_op jit(solution)/shard_map/all_gather | solution.py:109
  550.3 3.2 reduce.2
  556.2 2.4 copy.562
  (378 shorter events, 132.5 us)
Async XLA Ops:
  7.2 87.0 %copy-start = (bf16[1,32,4,16,128]{4,3,2,1,0:T(8,128)(2,1)S(1)}, bf16[1,32,4,16,128]{4,3,2,1,0:T(8,128)(2,1)}, u32[]{:S(2)}) copy-start(bf16[1,32,4,16,128]{4,3,2,1,0:T(8,128)(2,1)} %param.7) | copy-start | bytes 1572868
  7.2 231.4 %all-reduce.7.cloned.1.call-start = ((), (), s32[]{:S(2)}) async-start(), calls=%async_computation | async-start | bytes 884736 | tf_op jit(solution)/shard_map/psum | solution.py:98
  9.5 23.3 %collective-permute-start.1 = (bf16[1,128,1,512]{3,2,1,0:T(2,128)(2,1)}, bf16[1,128,1,512]{3,2,1,0:T(2,128)(2,1)S(1)}, u32[]{:S(2)}, u32[]{:S(2)}) collective-permute-start(bf16[1,128,1,512]{3,2,1,0:T(2,128)(2,1)} %get-tuple-element.123), channel_id=1, source_target_pairs={{4,0},{5,1},{6,2},{7,3},{12,8},{13,9},{14,10},{15,11},{20,16},{21,... | collective-permute-start | bytes 393224 | tf_op jit(solution)/shard_map/ppermute | solution.py:21
  10.8 9.6 %copy-start.67 = (f32[64,864]{1,0:T(8,128)S(1)}, f32[64,864]{1,0:T(8,128)}, u32[]{:S(2)}) copy-start(f32[64,864]{1,0:T(8,128)} %param.10) | copy-start | bytes 663556
  10.8 22.0 %collective-permute-start = (bf16[1,128,1,512]{3,2,1,0:T(2,128)(2,1)}, bf16[1,128,1,512]{3,2,1,0:T(2,128)(2,1)S(1)}, u32[]{:S(2)}, u32[]{:S(2)}) collective-permute-start(bf16[1,128,1,512]{3,2,1,0:T(2,128)(2,1)} %get-tuple-element.122), channel_id=1, source_target_pairs={{0,4},{1,5},{2,6},{3,7},{8,12},{9,13},{10,14},{11,15},{16,20},{17,... | collective-permute-start | bytes 393224 | tf_op jit(solution)/shard_map/ppermute | solution.py:20
  33.4 7.5 %collective-permute-start.3 = (bf16[1,128,4,64]{3,2,1,0:T(4,128)(2,1)S(1)}, bf16[1,128,4,64]{3,2,1,0:T(4,128)(2,1)S(1)}, u32[]{:S(2)}, u32[]{:S(2)}) collective-permute-start(bf16[1,128,4,64]{3,2,1,0:T(4,128)(2,1)S(1)} %get-tuple-element.38), channel_id=1, source_target_pairs={{1,0},{2,1},{3,2},{5,4},{6,5},{7,6},{9,8},{10,9},{11,10},{13,12},{... | collective-permute-start | bytes 196616 | tf_op jit(solution)/shard_map/ppermute | solution.py:21
  34.7 7.7 %collective-permute-start.2 = (bf16[1,128,4,64]{3,2,1,0:T(4,128)(2,1)S(1)}, bf16[1,128,4,64]{3,2,1,0:T(4,128)(2,1)S(1)}, u32[]{:S(2)}, u32[]{:S(2)}) collective-permute-start(bf16[1,128,4,64]{3,2,1,0:T(4,128)(2,1)S(1)} %get-tuple-element.37), channel_id=1, source_target_pairs={{0,1},{1,2},{2,3},{4,5},{5,6},{6,7},{8,9},{9,10},{10,11},{12,13},{... | collective-permute-start | bytes 196616 | tf_op jit(solution)/shard_map/ppermute | solution.py:20
  49.5 8.6 %copy-start.49 = (bf16[128,2,512]{2,1,0:T(2,128)(2,1)}, bf16[128,2,512]{2,1,0:T(2,128)(2,1)S(1)}, u32[]{:S(2)}) copy-start(bf16[128,2,512]{2,1,0:T(2,128)(2,1)S(1)} %get-tuple-element.65) | copy-start | bytes 786436
  49.5 9.2 %copy-start.31 = (bf16[128,2,512]{2,1,0:T(2,128)(2,1)}, bf16[128,2,512]{2,1,0:T(2,128)(2,1)S(1)}, u32[]{:S(2)}) copy-start(bf16[128,2,512]{2,1,0:T(2,128)(2,1)S(1)} %get-tuple-element.58) | copy-start | bytes 786436
  49.5 9.9 %copy-start.25 = (bf16[128,2,512]{2,1,0:T(2,128)(2,1)}, bf16[128,2,512]{2,1,0:T(2,128)(2,1)S(1)}, u32[]{:S(2)}) copy-start(bf16[128,2,512]{2,1,0:T(2,128)(2,1)S(1)} %get-tuple-element.59) | copy-start | bytes 786436
  49.5 10.5 %copy-start.21 = (bf16[128,2,512]{2,1,0:T(2,128)(2,1)}, bf16[128,2,512]{2,1,0:T(2,128)(2,1)S(1)}, u32[]{:S(2)}) copy-start(bf16[128,2,512]{2,1,0:T(2,128)(2,1)S(1)} %get-tuple-element.60) | copy-start | bytes 786436
  49.5 11.1 %copy-start.15 = (bf16[128,2,512]{2,1,0:T(2,128)(2,1)}, bf16[128,2,512]{2,1,0:T(2,128)(2,1)S(1)}, u32[]{:S(2)}) copy-start(bf16[128,2,512]{2,1,0:T(2,128)(2,1)S(1)} %get-tuple-element.61) | copy-start | bytes 786436
  49.6 11.8 %copy-start.11 = (bf16[128,2,512]{2,1,0:T(2,128)(2,1)}, bf16[128,2,512]{2,1,0:T(2,128)(2,1)S(1)}, u32[]{:S(2)}) copy-start(bf16[128,2,512]{2,1,0:T(2,128)(2,1)S(1)} %get-tuple-element.62) | copy-start | bytes 786436
  49.6 12.6 %copy-start.5 = (bf16[128,2,512]{2,1,0:T(2,128)(2,1)}, bf16[128,2,512]{2,1,0:T(2,128)(2,1)S(1)}, u32[]{:S(2)}) copy-start(bf16[128,2,512]{2,1,0:T(2,128)(2,1)S(1)} %get-tuple-element.64) | copy-start | bytes 786436
  49.6 13.2 %copy-start.3 = (bf16[128,2,512]{2,1,0:T(2,128)(2,1)}, bf16[128,2,512]{2,1,0:T(2,128)(2,1)S(1)}, u32[]{:S(2)}) copy-start(bf16[128,2,512]{2,1,0:T(2,128)(2,1)S(1)} %get-tuple-element.57) | copy-start | bytes 786436
  72.6 12.6 %collective-permute-start.5 = (bf16[1,64,1,16,128]{4,1,3,2,0:T(8,128)(2,1)S(1)}, bf16[1,64,1,16,128]{4,1,3,2,0:T(8,128)(2,1)S(1)}, u32[]{:S(2)}, u32[]{:S(2)}) collective-permute-start(bf16[1,64,1,16,128]{4,1,3,2,0:T(8,128)(2,1)S(1)} %get-tuple-element.32), channel_id=1, source_target_pairs={{4,0},{5,1},{6,2},{7,3},{12,8},{13,9},{14,10},{15,11},{20,16},{21,... | collective-permute-start | bytes 786440 | tf_op jit(solution)/shard_map/ppermute | solution.py:21
  74.1 11.2 %collective-permute-start.4 = (bf16[1,64,1,16,128]{4,1,3,2,0:T(8,128)(2,1)S(1)}, bf16[1,64,1,16,128]{4,1,3,2,0:T(8,128)(2,1)S(1)}, u32[]{:S(2)}, u32[]{:S(2)}) collective-permute-start(bf16[1,64,1,16,128]{4,1,3,2,0:T(8,128)(2,1)S(1)} %get-tuple-element.31), channel_id=1, source_target_pairs={{0,4},{1,5},{2,6},{3,7},{8,12},{9,13},{10,14},{11,15},{16,20},{17,... | collective-permute-start | bytes 786440 | tf_op jit(solution)/shard_map/ppermute | solution.py:20
  85.3 6.9 %collective-permute-start.7 = (bf16[1,64,6,1,128]{4,1,3,2,0:T(8,128)(2,1)S(1)}, bf16[1,64,6,1,128]{4,1,3,2,0:T(8,128)(2,1)S(1)}, u32[]{:S(2)}, u32[]{:S(2)}) collective-permute-start(bf16[1,64,6,1,128]{4,1,3,2,0:T(8,128)(2,1)S(1)} %get-tuple-element.30), channel_id=1, source_target_pairs={{1,0},{2,1},{3,2},{5,4},{6,5},{7,6},{9,8},{10,9},{11,10},{13,12},{... | collective-permute-start | bytes 294920 | tf_op jit(solution)/shard_map/ppermute | solution.py:21
  86.6 7.2 %collective-permute-start.6 = (bf16[1,64,6,1,128]{4,1,3,2,0:T(8,128)(2,1)S(1)}, bf16[1,64,6,1,128]{4,1,3,2,0:T(8,128)(2,1)S(1)}, u32[]{:S(2)}, u32[]{:S(2)}) collective-permute-start(bf16[1,64,6,1,128]{4,1,3,2,0:T(8,128)(2,1)S(1)} %get-tuple-element.29), channel_id=1, source_target_pairs={{0,1},{1,2},{2,3},{4,5},{5,6},{6,7},{8,9},{9,10},{10,11},{12,13},{... | collective-permute-start | bytes 294920 | tf_op jit(solution)/shard_map/ppermute | solution.py:20
  110.6 266.3 %all-reduce.9.cloned.1.call-start = ((), (), s32[]{:S(2)}) async-start(), calls=%async_computation.1 | async-start | bytes 2211840
  114.2 127.2 %copy-start.96 = (f32[1728]{0:T(1024)S(1)}, f32[1728]{0:T(1024)}, u32[]{:S(2)}) copy-start(f32[1728]{0:T(1024)} %param.12) | copy-start | bytes 20740
  241.4 136.6 %copy-start.68 = (f32[64,864]{1,0:T(8,128)S(1)}, f32[64,864]{1,0:T(8,128)}, u32[]{:S(2)}) copy-start(f32[64,864]{1,0:T(8,128)} %param.10) | copy-start | bytes 663556
  457.2 11.9 %copy-start.69 = (f32[128,1728]{0,1:T(8,128)S(1)}, f32[128,1728]{0,1:T(8,128)}, u32[]{:S(2)}) copy-start(f32[128,1728]{0,1:T(8,128)} %get-tuple-element.26) | copy-start | bytes 2654212
  475.3 79.9 %copy-start.71 = (f32[6912]{0:T(1024)}, f32[6912]{0:T(1024)S(1)}, u32[]{:S(2)}) copy-start(f32[6912]{0:T(1024)S(1)} %multiply_add_fusion) | copy-start | bytes 82948
  (83 other events, 253.6 us)
Sparse Core Ops, SparseCore 0:
  110.7 127.7 all-reduce.6
  245.5 131.2 all-reduce.8
where the time goes:
time: 574 us; the launch traced here: 566 us
  waiting for transfers between devices  258 us (45%)
  local copies, waits for them, and re-layouts  75 us (13%)
  blocking collectives  75 us (13%)
  matrix products  74.5 us (13%)
  other arithmetic  38.9 us (7%)
  starting transfers between devices  25.4 us (4%)
  between operations  19.2 us (3%)
    unnamed x3, waiting for transfers between devices  132 us
    psum x1, waiting for transfers between devices, local(): lax.psum((part_two, part_three), ('dp', 'depth', 'height'))  122 us
    all_gather x1, blocking collectives, local(): lax.all_gather(new_moment_three, ('dp', 'depth', 'height'), axis=0, tiled...  75 us
    dot_general x27, matrix products, local(): jnp.einsum('oi,odhw->idhw', wb_two[:, :, k], piece, preferred_element_typ...  47.4 us
    unnamed x226, local copies, waits for them, and re-layouts  39.1 us
    ppermute x4, starting transfers between devices, padded_2(): before = lax.ppermute(last, axis, up)  20 us
    dot_general x27, matrix products, local(): jnp.einsum('odhw,idhw->oi', piece, act_local, preferred_element_type=jnp....  15.2 us
    select_n x3, other arithmetic, local(): piece = jnp.where(inside, piece, jnp.zeros_like(piece))  12.6 us
  transfers between devices with their start and end apart: 10, of which 6 were waited for; matrix products, arithmetic and copies ran while one was open for 5% of the time, Pallas kernels for 0%

commit v1 on v0

v1 whole, which is shorter than its diff:
```python
import functools

import jax
import jax.numpy as jnp
from jax import lax
from jax.experimental import pallas as pl
from jax.experimental.pallas import tpu as pltpu
from jax.sharding import PartitionSpec as P

AXES = ("dp", "depth", "height")
MESH = pl.DeviceIdType.MESH

SLOPE = 0.3
LEARN = 4.0
TRUST = 0.05
MOMENTUM = 0.9
EPSILON = 1e-06


def leaky(value):
    return jnp.where(value > 0, value, SLOPE * value)


def slope_of(value):
    return jnp.where(value > 0, 1.0, SLOPE).astype(jnp.float32)


def dot(a, b):
    return jnp.dot(a, b, preferred_element_type=jnp.float32)


def dot_t(a, b):
    return lax.dot_general(a, b, (((1,), (1,)), ((), ())), preferred_element_type=jnp.float32)


def step_kernel(
    half_w, scales, rates, cot_ref, pre_ref, act_ref, w2_ref, w3_ref, m2_ref, m3_ref,
    gin_ref, new2_ref, new3_ref, mom2_ref, mom3_ref,
    cot_x, pre_x, perm3, perm2, wide3, wide2, taps3, taps2, back_acc, upper, act_wide, pool_wide,
    into, g2_acc, g3_acc, squared, *rest,
):
    layer_refs, (send_sem, recv_sem, own_sem) = (rest[:-3], rest[-3:])
    per_layer = len(layer_refs) // 2
    names = ("parts", "recv_a", "send_b", "recv_b", "send_c", "recv_c", "moments", "full")
    layer2 = dict(zip(names, layer_refs[:per_layer]))
    layer3 = dict(zip(names, layer_refs[per_layer:]))
    me = [lax.axis_index(name) for name in AXES]
    sizes = [lax.axis_size(name) for name in AXES]
    last = [size - 1 for size in sizes]
    used = [0]

    def device(axis, index):
        return tuple(index if i == axis else me[i] for i in range(3))

    def others(axis):
        return [lax.rem(me[axis] + step, sizes[axis]) for step in range(1, sizes[axis])]

    def remote(source, target, to):
        n = used[0]
        used[0] += 1
        return pltpu.make_async_remote_copy(
            src_ref=source, dst_ref=target, send_sem=send_sem.at[n], recv_sem=recv_sem.at[n],
            device_id=to, device_id_type=MESH,
        )

    def send(axis, source, target):
        copies = []
        for j, other in enumerate(others(axis)):
            copy = remote(source(other), target(j), device(axis, other))
            copy.start()
            copies.append(copy)
        return copies

    def finish(copies):
        for copy in copies:
            copy.wait()

    sides = [(d, h) for d in (-1, 0, 1) for h in (-1, 0, 1) if (d, h) != (0, 0)]

    def present(d, h):
        down, along = (me[1] + d, me[2] + h)
        return (down >= 0) & (down <= last[1]) & (along >= 0) & (along <= last[2])

    def part(side, length, width, taken):
        if side == 0:
            return pl.ds(0 if taken else width, length)
        if taken:
            return pl.ds(length - width if side > 0 else 0, width)
        return pl.ds(0 if side > 0 else width + length, width)

    arrays = ((cot_ref, cot_x, (2, 2 * half_w)), (pre_ref, pre_x, (1, 2 * half_w)))

    def place(ref, width, d, h, taken):
        layers, _, lanes = ref.shape
        return (part(d, layers, width[0], taken), slice(None), part(h, lanes, width[1], taken))

    barrier = pltpu.get_barrier_semaphore()

    def greet(to):
        pl.semaphore_signal(barrier, inc=1, device_id=to, device_id_type=MESH)

    for i in range(sizes[0]):
        for j in range(sizes[1]):
            if i or j:
                a, b = (lax.rem(me[0] + i, sizes[0]), lax.rem(me[1] + j, sizes[1]))
                greet((a, b, me[2]))
    for other in others(2):
        greet(device(2, other))
    for d, h in sides:
        if d and h:
            @pl.when(present(d, h))
            def _():
                greet((me[0], me[1] + d, me[2] + h))
    around = [jnp.where(me[i] > 0, 1, 0) + jnp.where(me[i] < last[i], 1, 0) for i in (1, 2)]
    pl.semaphore_wait(barrier, sizes[0] * sizes[1] + sizes[2] - 2 + around[0] * around[1])

    edges = [[], []]
    for a, (ref, out, width) in enumerate(arrays):
        for d, h in sides:
            copy = remote(
                ref.at[place(ref, width, d, h, True)], out.at[place(ref, width, d, h, False)],
                (me[0], me[1] + d, me[2] + h),
            )
            edges[a].append((d, h, copy))

            @pl.when(present(d, h))
            def _():
                copy.start()

    own = []
    for a, (ref, out, width) in enumerate(arrays):
        copy = pltpu.make_async_copy(ref, out.at[place(ref, width, 0, 0, False)], own_sem.at[a])
        copy.start()
        own.append(copy)
    moment_copies = []
    for layer, ref in ((layer2, m2_ref), (layer3, m3_ref)):
        layer["moments"][me[2]] = ref[...]
        moment_copies += send(
            2, lambda other: ref, lambda j: layer["moments"].at[me[2]]
        )
    for d, h in sides:
        @pl.when(jnp.logical_not(present(-d, -h)))
        def _():
            for ref, out, width in arrays:
                where = place(ref, width, d, h, False)
                shape = (where[0].size, ref.shape[1], where[2].size)
                out[where] = jnp.zeros(shape, out.dtype)

    def finish_edges(a):
        own[a].wait()
        for d, h, copy in edges[a]:
            @pl.when(present(d, h))
            def _():
                copy.wait_send()

            @pl.when(present(-d, -h))
            def _():
                copy.wait_recv()

    bf16, f32 = (jnp.bfloat16, jnp.float32)
    chan_three, chan_two, chan_one = (cot_x.shape[1], pre_x.shape[1], act_ref.shape[1])
    wide = 2 * half_w
    layers3, lanes3 = (cot_x.shape[0], cot_x.shape[2])
    inner3 = lanes3 - wide
    layers2, lanes2 = (pre_x.shape[0], pre_x.shape[2])
    own_layers, own_lanes = act_ref.shape[0], act_ref.shape[2]
    rows2 = lanes2 // wide
    iota = lambda shape, dim: lax.broadcasted_iota(jnp.int32, shape, dim)
    depth, height = (me[1], me[2])
    one = lambda flag: jnp.where(flag, 1.0, 0.0).astype(f32)
    above, below = (one(depth > 0), one(depth < sizes[1] - 1))
    left, right = (one(height > 0), one(height < sizes[2] - 1))

    n3, n2 = (3 * chan_two, 3 * chan_one)
    row3, col3 = (iota((n3, 1), 0), iota((1, 27 * chan_two), 1))
    row2, col2 = (iota((n2, 1), 0), iota((1, 27 * chan_one), 1))
    for t in range(9):
        aim = (row3 % chan_two) * 27 + (row3 // chan_two) * 9 + t
        perm3[t] = jnp.where(col3 == aim, 1.0, 0.0).astype(bf16)
        aim = (row2 % chan_one) * 27 + (t // 3) * 9 + (row2 // chan_one) * 3 + t % 3
        perm2[t] = jnp.where(col2 == aim, 1.0, 0.0).astype(bf16)
    w3, w2 = (w3_ref[...].astype(bf16), w2_ref[...].astype(bf16))
    for t in range(9):
        taps3[:, t * chan_three : (t + 1) * chan_three] = dot_t(perm3[t], w3).astype(bf16)
    for kd in range(3):
        taps2[kd * n2 : (kd + 1) * n2, :] = jnp.concatenate(
            [dot_t(perm2[kd * 3 + kw], w2) for kw in range(3)], axis=1
        ).astype(bf16)

    norms = [
        jnp.sqrt(jnp.sum(jnp.sum(w * w, axis=0, keepdims=True), axis=1, keepdims=True))
        for w in (w2_ref[...], w3_ref[...])
    ]
    halves = jnp.where(iota((2 * wide, wide), 0) // 2 == iota((2 * wide, wide), 1), 0.125, 0.0)
    halves = halves.astype(bf16)
    coarse = own_layers // 2
    pool_wide[...] = jnp.zeros_like(pool_wide)
    for d in range(coarse):
        total = leaky(pre_ref[2 * d].astype(f32)) + leaky(pre_ref[2 * d + 1].astype(f32))
        coarse_rows = inner3 // half_w
        sums = []
        for q in range(coarse_rows):
            if q in (0, coarse_rows - 1):
                sums.append(jnp.zeros((chan_two, wide), f32))
            else:
                at = (2 * q - 2) * wide
                sums.append(total[:, at : at + wide] + total[:, at + wide : at + 2 * wide])
        for pair in range(coarse_rows // 2):
            both = jnp.concatenate(sums[2 * pair : 2 * pair + 2], axis=1)
            high = both.astype(bf16)
            low = (both - high.astype(f32)).astype(bf16)
            mean = (dot(high, halves) + dot(low, halves)).astype(bf16)
            for kd in range(3):
                pool_wide[
                    d + 2 - kd, kd * chan_two : (kd + 1) * chan_two, pair * wide : (pair + 1) * wide
                ] = mean

    finish_edges(0)

    back_acc[...] = jnp.zeros_like(back_acc)
    column3 = iota((1, lanes3), 1) % half_w

    @pl.loop(0, layers3)
    def _(e):
        whole = cot_x[e].astype(f32)
        for kw in range(3):
            ow = 2 - kw
            moved = whole
            if ow == 0:
                moved = jnp.where(column3 == 0, 0.0, pltpu.roll(whole, 1, 1))
            elif ow == 2:
                moved = jnp.where(column3 == half_w - 1, 0.0, pltpu.roll(whole, lanes3 - 1, 1))
            for kh in range(3):
                start = (2 - kh) * half_w
                piece = moved if start == 0 else pltpu.roll(moved, lanes3 - start, 1)
                t = kh * 3 + kw
                wide3[e, t * chan_three : (t + 1) * chan_three, :] = piece[:, :inner3].astype(bf16)
        product = dot(taps3[...], wide3[e])
        for kd in range(3):
            back_acc[e + kd] += product[kd * chan_two : (kd + 1) * chan_two]

    twice = jnp.where(iota((wide, 2 * wide), 0) == iota((wide, 2 * wide), 1) // 2, 1.0, 0.0)
    twice = twice.astype(bf16)
    for layer in range(layers3 - 2):
        cells = (scales[1] * back_acc[layer + 2]).astype(bf16)
        for pair in range(inner3 // wide):
            upper[layer, :, pair * 2 * wide : (pair + 1) * 2 * wide] = dot(
                cells[:, pair * wide : (pair + 1) * wide], twice
            )

    for t in range(9):
        rows = slice(t * chan_three, (t + 1) * chan_three)
        grad = dot_t(wide3[1, rows, :], pool_wide[0])
        for e in range(1, coarse + 2):
            grad = grad + dot_t(wide3[e + 1, rows, :], pool_wide[e])
        ordered = dot(grad.astype(bf16), perm3[t])
        if t == 0:
            g3_acc[...] = ordered
        else:
            g3_acc[...] += ordered

    def first_sum(layer, acc):
        parts = layer["parts"]
        rows = parts.shape[2]
        for i in range(sizes[0]):
            for j in range(sizes[1]):
                at = (i * sizes[1] + j) * rows
                parts[i, j] = acc[at : at + rows].astype(bf16)
        return send(0, lambda other: parts.at[other], lambda j: layer["recv_a"].at[j])

    def second_sum(layer, copies):
        finish(copies)
        total = layer["parts"][me[0]].astype(f32)
        for j in range(sizes[0] - 1):
            total = total + layer["recv_a"][j].astype(f32)
        layer["send_b"][...] = total.astype(bf16)
        return send(
            1, lambda other: layer["send_b"].at[other], lambda j: layer["recv_b"].at[j]
        )

    def third_sum(layer, copies):
        finish(copies)
        total = layer["send_b"][me[1]].astype(f32)
        for j in range(sizes[1] - 1):
            total = total + layer["recv_b"][j].astype(f32)
        layer["send_c"][...] = total.astype(bf16)
        layer["recv_c"][me[2]] = layer["send_c"][...]
        return send(2, lambda other: layer["send_c"], lambda j: layer["recv_c"].at[me[2]])

    def summed(layer, copies, rate):
        finish(copies)
        total = layer["recv_c"][0].astype(f32)
        for j in range(1, sizes[2]):
            total = total + layer["recv_c"][j].astype(f32)
        return total * rate

    copies3 = first_sum(layer3, g3_acc)
    finish_edges(1)

    column2 = iota((1, lanes2), 1) % wide
    lane = iota((1, lanes2), 1)
    edge = jnp.where(lane < wide, left, jnp.where(lane >= lanes2 - wide, right, 1.0))
    into[...] = jnp.zeros_like(into)

    @pl.loop(0, layers2)
    def _(f):
        parent = upper[(f + 1) // 2]
        cells = [parent[:, (r + 1) // 2 * wide : ((r + 1) // 2 + 1) * wide] for r in range(rows2)]
        spread = jnp.concatenate(cells, axis=1)
        inside = edge * jnp.where(f == 0, above, jnp.where(f == layers2 - 1, below, 1.0))
        value = spread * 0.125 * slope_of(pre_x[f].astype(f32))
        value = jnp.where(inside > 0, value, 0.0)
        before = jnp.where(column2 == 0, 0.0, pltpu.roll(value, 1, 1))
        after = jnp.where(column2 == wide - 1, 0.0, pltpu.roll(value, lanes2 - 1, 1))
        for kw, moved in enumerate((after, value, before)):
            wide2[f, kw * chan_two : (kw + 1) * chan_two, :] = moved.astype(bf16)
        product = dot(taps2[...], wide2[f])
        for kd in range(3):
            total = None
            for kh in range(3):
                at, start = ((kd * 3 + kh) * chan_one, (2 - kh) * wide)
                term = product[at : at + chan_one, start : start + own_lanes]
                total = term if total is None else total + term
            into[f + kd] += total

    copies3 = second_sum(layer3, copies3)

    act_wide[...] = jnp.zeros_like(act_wide)
    for d in range(own_layers):
        for kh in range(3):
            start = (2 - kh) * wide
            act_wide[d, kh * chan_one : (kh + 1) * chan_one, start : start + own_lanes] = act_ref[d]
    n_wide = 3 * chan_two
    for kd in range(3):
        grad = dot_t(wide2[2 - kd], act_wide[0])
        for d in range(1, own_layers):
            grad = grad + dot_t(wide2[d + 2 - kd], act_wide[d])
        grad = grad.astype(bf16)
        for kw in range(3):
            ordered = dot(grad[kw * chan_two : (kw + 1) * chan_two], perm2[kd * 3 + kw])
            if kd == 0 and kw == 0:
                g2_acc[...] = ordered
            else:
                g2_acc[...] += ordered

    copies2 = first_sum(layer2, g2_acc)
    copies3 = third_sum(layer3, copies3)
    for d in range(own_layers):
        gin_ref[d] = (scales[0] * into[d + 2]).astype(bf16)
    finish(moment_copies)
    copies2 = second_sum(layer2, copies2)
    grad_three = summed(layer3, copies3, rates[1])
    copies2 = third_sum(layer2, copies2)
    grad_two = summed(layer2, copies2, rates[0])

    squares = [
        jnp.sum(jnp.sum(g * g, axis=0, keepdims=True), axis=1, keepdims=True)
        for g in (grad_two, grad_three)
    ]
    line = lax.broadcasted_iota(jnp.int32, (8, 128), 0)
    slot = me[0] * sizes[1] + me[1]
    squared[slot] = jnp.where(line == 0, squares[0], squares[1])
    copies = []
    for i in range(sizes[0]):
        for j in range(sizes[1]):
            if i or j:
                a, b = (lax.rem(me[0] + i, sizes[0]), lax.rem(me[1] + j, sizes[1]))
                copy = remote(squared.at[slot], squared.at[slot], (a, b, me[2]))
                copy.start()
                copies.append(copy)
    finish(copies)
    total = squared[0]
    for n in range(1, sizes[0] * sizes[1]):
        total = total + squared[n]
    norm_g = jnp.sqrt(total)
    copies = []
    layers = ((layer2, grad_two, mom2_ref), (layer3, grad_three, mom3_ref))
    for n, (layer, grad, mom_ref) in enumerate(layers):
        trust = TRUST * norms[n] / (norm_g[n : n + 1, 0:1] + EPSILON)
        pieces = [layer["moments"][c] for c in range(sizes[2])]
        split = grad.shape[1] // pieces[0].shape[1]
        lines = [
            pieces[c] if split == 1 else jnp.concatenate(pieces[c : c + split], axis=1)
            for c in range(0, sizes[2], split)
        ]
        old = lines[0] if len(lines) == 1 else jnp.concatenate(lines, axis=0)
        moment = MOMENTUM * old + LEARN * trust * grad
        mom_ref[...] = moment
        full = layer["full"]
        full[me[0], me[1]] = moment.astype(bf16)
        copies.append(send(
            1, lambda other: full.at[me[0], me[1]], lambda j: full.at[me[0], me[1]]
        ))

    again = []
    for (layer, _, _), sent in zip(layers, copies):
        full = layer["full"]
        finish(sent)
        again.append(send(0, lambda other: full.at[me[0]], lambda j: full.at[me[0]]))
    targets = ((w2_ref, new2_ref), (w3_ref, new3_ref))
    for (layer, _, _), sent, (w_ref, new_ref) in zip(layers, again, targets):
        full = layer["full"]
        finish(sent)
        rows = full.shape[2]
        for i in range(sizes[0]):
            for j in range(sizes[1]):
                at = (i * sizes[1] + j) * rows
                new_ref[at : at + rows, :] = w_ref[at : at + rows, :] - full[i, j].astype(f32)


def local(act_one, pre_two, cot_three, weight_two, weight_three, moment_two, moment_three):
    chan_one, chan_two, chan_three = (act_one.shape[1], pre_two.shape[1], cot_three.shape[1])
    local_d, local_h, local_w = pre_two.shape[2:]
    half_w = local_w // 2
    sizes = tuple(lax.axis_size(name) for name in AXES)
    scale_two = (chan_one * 27) ** (-0.5)
    scale_three = (chan_two * 27) ** (-0.5)
    bf16, f32 = (jnp.bfloat16, jnp.float32)

    def by_layer(x):
        return x[0].reshape(x.shape[1], x.shape[2], -1).transpose(1, 0, 2)

    act, cot, pre = (by_layer(act_one), by_layer(cot_three), by_layer(pre_two))
    layers3, lanes3 = (cot.shape[0] + 4, cot.shape[2] + 4 * half_w)
    layers2, lanes2 = (pre.shape[0] + 2, pre.shape[2] + 2 * local_w)
    inner3 = lanes3 - 2 * half_w
    held, blocks, moments = ([], [], [])
    for weight, moment in ((weight_two, moment_two), (weight_three, moment_three)):
        rows, width = (weight.shape[0] // (sizes[0] * sizes[1]), weight.shape[1])
        line = min(width, moment.shape[0])
        moments.append(moment.reshape(-1, line))
        blocks.append(jax.ShapeDtypeStruct((rows, width), f32))
        held += [
            pltpu.VMEM((sizes[0], sizes[1], rows, width), bf16),
            pltpu.VMEM((sizes[0] - 1, sizes[1], rows, width), bf16),
            pltpu.VMEM((sizes[1], rows, width), bf16),
            pltpu.VMEM((sizes[1] - 1, rows, width), bf16),
            pltpu.VMEM((rows, width), bf16),
            pltpu.VMEM((sizes[2], rows, width), bf16),
            pltpu.VMEM((sizes[2],) + moments[-1].shape, f32),
            pltpu.VMEM((sizes[0], sizes[1], rows, width), bf16),
        ]
    copies = 16 + 4 * (sum(sizes) - 3) + 2 * (sizes[2] - 1) + sizes[0] * sizes[1] - 1
    vmem = pl.BlockSpec(memory_space=pltpu.VMEM)
    grad_input, new_weight_two, new_weight_three, block_two, block_three = pl.pallas_call(
        functools.partial(
            step_kernel, half_w, (scale_two, scale_three),
            (scale_two / sizes[0], scale_three / sizes[0]),
        ),
        out_shape=(
            jax.ShapeDtypeStruct(act.shape, bf16),
            jax.ShapeDtypeStruct(weight_two.shape, f32),
            jax.ShapeDtypeStruct(weight_three.shape, f32),
            *blocks,
        ),
        in_specs=[vmem] * 7,
        out_specs=(vmem,) * 5,
        scratch_shapes=[
            pltpu.VMEM((layers3, chan_three, lanes3), bf16),
            pltpu.VMEM((layers2, chan_two, lanes2), bf16),
            pltpu.VMEM((9, 3 * chan_two, 27 * chan_two), bf16),
            pltpu.VMEM((9, 3 * chan_one, 27 * chan_one), bf16),
            pltpu.VMEM((layers3, 9 * chan_three, inner3), bf16),
            pltpu.VMEM((layers2, 3 * chan_two, lanes2), bf16),
            pltpu.VMEM((3 * chan_two, 9 * chan_three), bf16),
            pltpu.VMEM((9 * chan_one, 3 * chan_two), bf16),
            pltpu.VMEM((layers3 + 2, chan_two, inner3), f32),
            pltpu.VMEM((layers3 - 2, chan_two, 2 * inner3), f32),
            pltpu.VMEM((local_d, 3 * chan_one, lanes2), bf16),
            pltpu.VMEM((local_d // 2 + 2, 3 * chan_two, inner3), bf16),
            pltpu.VMEM((layers2 + 2, chan_one, act.shape[2]), f32),
            pltpu.VMEM(weight_two.shape, f32),
            pltpu.VMEM(weight_three.shape, f32),
            pltpu.VMEM((sizes[0] * sizes[1], 8, 128), f32),
            *held,
            pltpu.SemaphoreType.DMA((copies,)),
            pltpu.SemaphoreType.DMA((copies,)),
            pltpu.SemaphoreType.DMA((2,)),
        ],
        compiler_params=pltpu.CompilerParams(
            collective_id=0, has_side_effects=True, vmem_limit_bytes=56 * 2**20
        ),
        name="step",
    )(cot, pre, act, weight_two, weight_three, *moments)
    grad_input = grad_input.transpose(1, 0, 2).reshape(act_one.shape)
    mine = lax.axis_index("height")
    new_moment_two, new_moment_three = (
        lax.dynamic_slice_in_dim(block.reshape(-1), mine * moment.shape[0], moment.shape[0])
        for block, moment in ((block_two, moment_two), (block_three, moment_three))
    )
    return (grad_input, new_weight_two, new_weight_three, new_moment_two, new_moment_three)


def solution(mesh):
    in_specs = (
        P("dp", None, "depth", "height", None),
        P("dp", None, "depth", "height", None),
        P("dp", None, "depth", "height"),
        P(),
        P(),
        P(("dp", "depth", "height")),
        P(("dp", "depth", "height")),
    )
    out_specs = (
        P("dp", None, "depth", "height", None),
        P(),
        P(),
        P(("dp", "depth", "height")),
        P(("dp", "depth", "height")),
    )
    return jax.shard_map(local, mesh=mesh, in_specs=in_specs, out_specs=out_specs, check_vma=False)
```

time: 574 us -> 84.1 us (0.15); the launches traced: 566 us -> 83 us
  waiting for transfers between devices: 258 us -> 0 us
  blocking collectives: 75 us -> 0 us
  matrix products: 74.5 us -> 0 us
  Pallas kernels: 0 us -> 68.4 us
  local copies, waits for them, and re-layouts: 75 us -> 14 us
  other arithmetic: 38.9 us -> 0 us
  starting transfers between devices: 25.4 us -> 0 us
  between operations: 19.2 us -> 0.7 us
    unnamed x3 -> x0, waiting for transfers between devices: 132 us -> none
    psum x1 -> x0, waiting for transfers between devices: 122 us -> none  [local(): lax.psum((part_two, part_three), ('dp', 'depth', 'height'))]
    all_gather x1 -> x0, blocking collectives: 75 us -> none  [local(): lax.all_gather(new_moment_three, ('dp', 'depth', 'height'), axis=0, tiled...]
    dot_general x108 -> x0, matrix products: 74.5 us -> none  [the longest x27 47.4 us: local(): jnp.einsum('oi,odhw->idhw', wb_two[:, :, k], piece, preferred_element_typ...]
    pallas_call x0 -> x1, Pallas kernels: none -> 68.4 us  [local(): pl.pallas_call(functools.partial(step_kernel, half_w, (scale_two, scale_t...]
    unnamed x226 -> x22, local copies, waits for them, and re-layouts: 39.1 us -> 6.99 us
    ppermute x8 -> x0, starting transfers between devices: 25.3 us -> none  [the longest x4 20 us: padded_2(): before = lax.ppermute(last, axis, up)]
    slice x6 -> x0, local copies, waits for them, and re-layouts: 12.7 us -> none  [the longest x2 8.19 us: local(): wb_two[:, :, k]]
  transfers between devices with their start and end apart: 10 -> 0, of which waited for: 6 -> 0; matrix products, arithmetic and copies ran while one was open for 5% -> 0% of each run, Pallas kernels for 0% -> 0%
where the time goes in v1:
time: 84.1 us; the launch traced here: 83 us
  Pallas kernels  68.4 us (81%)
  local copies, waits for them, and re-layouts  14 us (17%)
    pallas_call x1, Pallas kernels, local(): pl.pallas_call(functools.partial(step_kernel, half_w, (scale_two, scale_t...  68.4 us
    unnamed x22, local copies, waits for them, and re-layouts  6.99 us
    another operation x4, local copies, waits for them, and re-layouts, by_layer(): return x[0].reshape(x.shape[1], x.shape[2], -1).transpose(1, 0, 2)  4.09 us

profile of v1, /device:TPU:0, one launch (start us, length us, event | category | flops | bytes accessed | tf_op | source)
XLA Modules:
  0.0 83.0 jit_solution(4196438406219093345)
XLA Ops:
  0.6 1.7 %copy.26 = bf16[1,128,2,512]{3,1,2,0:T(8,128)(2,1)} copy(bf16[1,128,2,512]{3,2,1,0:T(2,128)(2,1)} %param.9) | data formatting | bytes 524288 | tf_op args[2]
  2.3 1.3 %reshape.30 = bf16[64,4,2048]{2,1,0:T(4,128)(2,1)S(1)} reshape(bf16[1,64,4,16,128]{4,3,2,1,0:T(8,128)(2,1)} %param.8) | data formatting | bytes 2097152 | tf_op jit(solution)/shard_map/reshape;squeeze | solution.py:421
  3.7 0.0 copy-start.2
  3.7 1.5 %copy.24 = bf16[64,4,2048]{2,0,1:T(8,128)(2,1)} copy(bf16[64,4,2048]{2,1,0:T(4,128)(2,1)S(1)} %reshape.30) | data formatting | bytes 2097152 | tf_op jit(solution)/shard_map/reshape;squeeze | solution.py:421
  5.2 0.0 copy-done.2
  5.2 0.1 reshape.31
  5.3 1.1 %copy.25 = bf16[32,4,2048]{2,0,1:T(8,128)(2,1)} copy(bf16[32,4,2048]{2,1,0:T(4,128)(2,1)S(1)} %reshape.31) | data formatting | bytes 1048576 | tf_op jit(solution)/shard_map/reshape;squeeze | solution.py:421
  6.4 0.0 copy-done.1
  6.4 1.3 %copy.15.w3_ref = f32[128,1728]{1,0:T(8,128)} copy(f32[128,1728]{0,1:T(8,128)S(1)} %copy-done.1) | data formatting | bytes 1769472 | tf_op args[4]
  7.7 0.0 copy-done.7
  7.7 0.7 reshape.25.m2_ref
  8.4 0.0 copy-done.5
  8.4 0.7 reshape.26.m3_ref
  9.1 68.4 %step.1 = (bf16[4,32,2048]{2,1,0:T(8,128)(2,1)}, f32[64,864]{1,0:T(8,128)}, f32[128,1728]{1,0:T(8,128)}, f32[8,864]{1,0:T(8,128)}, f32[16,1728]{1,0:T(8,128)}) custom-call(bf16[2,128,512]{2,1,0:T(8,128)(2,1)} %bitcast.25, bf16[4,64,2048]{2,1,0:T(8,128)(2,1)} %bitcast.22, bf16[4,32,2048]{2,1,0:T(8,128)(2,1)} %bitcast.23, f32[64,864]{1,0:T(8,128)} %w2_ref.1, ...), custom_call_target="tpu_custom_call" | custom-call | tf_op jit(solution)/shard_map/step/pallas_call | solution.py:445
  77.5 0.0 copy-start
  77.5 1.2 %copy.20 = bf16[16,8,16,128]{3,2,1,0:T(8,128)(2,1)S(1)} copy(bf16[16,8,16,128]{3,1,2,0:T(8,128)(2,1)} %bitcast.26) | data formatting | bytes 1048576
  78.7 0.9 %copy.16 = bf16[1,32,4,16,128]{4,3,2,1,0:T(8,128)(2,1)} copy(bf16[1,32,4,16,128]{4,3,1,2,0:T(8,128)(2,1)S(1)} %bitcast.24) | data formatting | bytes 1048576
  79.6 1.2 %copy.17 = f32[128,1728]{0,1:T(8,128)} copy(f32[128,1728]{1,0:T(8,128)S(1)} %copy-done) | data formatting | bytes 1769472
  80.8 0.1 reshape.28
  80.9 0.7 dynamic_slice.6
  81.6 0.0 copy-done.4
  81.6 0.1 reshape.29
  81.7 0.7 dynamic_slice.7
  82.4 0.7 copy.28
  (9 shorter events, 0.0 us)
Async XLA Ops:
  3.7 1.6 %copy-start.2 = (bf16[1,32,4,16,128]{4,3,2,1,0:T(8,128)(2,1)S(1)}, bf16[1,32,4,16,128]{4,3,2,1,0:T(8,128)(2,1)}, u32[]{:S(2)}) copy-start(bf16[1,32,4,16,128]{4,3,2,1,0:T(8,128)(2,1)} %param.7) | copy-start | bytes 1572868
  5.2 1.2 %copy-start.1 = (f32[128,1728]{0,1:T(8,128)S(1)}, f32[128,1728]{0,1:T(8,128)}, u32[]{:S(2)}) copy-start(f32[128,1728]{0,1:T(8,128)} %param.11) | copy-start | bytes 2654212
  6.4 1.3 %copy-start.7 = (f32[1728]{0:T(1024)S(1)}, f32[1728]{0:T(1024)}, u32[]{:S(2)}) copy-start(f32[1728]{0:T(1024)} %param.12) | copy-start | bytes 20740
  6.4 2.0 %copy-start.5 = (f32[6912]{0:T(1024)S(1)}, f32[6912]{0:T(1024)}, u32[]{:S(2)}) copy-start(f32[6912]{0:T(1024)} %param.13) | copy-start | bytes 82948
  77.5 2.1 %copy-start = (f32[128,1728]{1,0:T(8,128)S(1)}, f32[128,1728]{1,0:T(8,128)}, u32[]{:S(2)}) copy-start(f32[128,1728]{1,0:T(8,128)} %get-tuple-element.17) | copy-start | bytes 2654212
  79.6 1.2 %copy-start.6 = (f32[8,864]{1,0:T(8,128)S(1)}, f32[8,864]{1,0:T(8,128)}, u32[]{:S(2)}) copy-start(f32[8,864]{1,0:T(8,128)} %get-tuple-element.13) | copy-start | bytes 82948
  79.6 2.0 %copy-start.4 = (f32[16,1728]{1,0:T(8,128)S(1)}, f32[16,1728]{1,0:T(8,128)}, u32[]{:S(2)}) copy-start(f32[16,1728]{1,0:T(8,128)} %get-tuple-element.14) | copy-start | bytes 331780
  80.8 1.6 %copy-start.3 = (f32[64,864]{1,0:T(8,128)S(1)}, f32[64,864]{1,0:T(8,128)}, u32[]{:S(2)}) copy-start(f32[64,864]{1,0:T(8,128)} %get-tuple-element.26) | copy-start | bytes 663556

commit v2 on v1

--- a/solution.py
+++ b/solution.py
@@ -29,6 +29,11 @@
     return jnp.dot(a, b, preferred_element_type=jnp.float32)
 
 
+def in_rows(ref, layer):
+    rows = [ref[layer, r].astype(jnp.float32) for r in range(ref.shape[1])]
+    return jnp.concatenate(rows, axis=1)
+
+
 def dot_t(a, b):
     return lax.dot_general(a, b, (((1,), (1,)), ((), ())), preferred_element_type=jnp.float32)
 
@@ -37,11 +42,11 @@
     half_w, scales, rates, cot_ref, pre_ref, act_ref, w2_ref, w3_ref, m2_ref, m3_ref,
     gin_ref, new2_ref, new3_ref, mom2_ref, mom3_ref,
     cot_x, pre_x, perm3, perm2, wide3, wide2, taps3, taps2, back_acc, upper, act_wide, pool_wide,
-    into, g2_acc, g3_acc, squared, *rest,
+    into, g2_acc, g3_acc, *rest,
 ):
     layer_refs, (send_sem, recv_sem, own_sem) = (rest[:-3], rest[-3:])
     per_layer = len(layer_refs) // 2
-    names = ("parts", "recv_a", "send_b", "recv_b", "send_c", "recv_c", "moments", "full")
+    names = ("parts", "arrived", "partial", "partials", "moments", "decayed", "full")
     layer2 = dict(zip(names, layer_refs[:per_layer]))
     layer3 = dict(zip(names, layer_refs[per_layer:]))
     me = [lax.axis_index(name) for name in AXES]
@@ -71,6 +76,19 @@
             copies.append(copy)
         return copies
 
+    peers = [
+        (lax.rem(me[0] + i, sizes[0]), lax.rem(me[1] + j, sizes[1]))
+        for i in range(sizes[0]) for j in range(sizes[1]) if i or j
+    ]
+
+    def send_all(source, target):
+        copies = []
+        for n, (a, b) in enumerate(peers):
+            copy = remote(source(a, b), target(n), (a, b, me[2]))
+            copy.start()
+            copies.append(copy)
+        return copies
+
     def finish(copies):
         for copy in copies:
             copy.wait()
@@ -88,22 +106,20 @@
             return pl.ds(length - width if side > 0 else 0, width)
         return pl.ds(0 if side > 0 else width + length, width)
 
-    arrays = ((cot_ref, cot_x, (2, 2 * half_w)), (pre_ref, pre_x, (1, 2 * half_w)))
+    arrays = ((cot_ref, cot_x, (2, 2 * half_w)), (pre_ref, pre_x, (1, 1)))
 
     def place(ref, width, d, h, taken):
-        layers, _, lanes = ref.shape
-        return (part(d, layers, width[0], taken), slice(None), part(h, lanes, width[1], taken))
+        layers, along = (ref.shape[0], ref.shape[1 if ref.ndim == 4 else 2])
+        where = (part(d, layers, width[0], taken), part(h, along, width[1], taken))
+        return where if ref.ndim == 4 else (where[0], slice(None), where[1])
 
     barrier = pltpu.get_barrier_semaphore()
 
     def greet(to):
         pl.semaphore_signal(barrier, inc=1, device_id=to, device_id_type=MESH)
 
-    for i in range(sizes[0]):
-        for j in range(sizes[1]):
-            if i or j:
-                a, b = (lax.rem(me[0] + i, sizes[0]), lax.rem(me[1] + j, sizes[1]))
-                greet((a, b, me[2]))
+    for a, b in peers:
+        greet((a, b, me[2]))
     for other in others(2):
         greet(device(2, other))
     for d, h in sides:
@@ -143,7 +159,10 @@
         def _():
             for ref, out, width in arrays:
                 where = place(ref, width, d, h, False)
-                shape = (where[0].size, ref.shape[1], where[2].size)
+                if ref.ndim == 4:
+                    shape = (where[0].size, where[1].size) + ref.shape[2:]
+                else:
+                    shape = (where[0].size, ref.shape[1], where[2].size)
                 out[where] = jnp.zeros(shape, out.dtype)
 
     def finish_edges(a):
@@ -158,12 +177,13 @@
                 copy.wait_recv()
 
     bf16, f32 = (jnp.bfloat16, jnp.float32)
-    chan_three, chan_two, chan_one = (cot_x.shape[1], pre_x.shape[1], act_ref.shape[1])
+    chan_three, chan_two, chan_one = (cot_x.shape[1], pre_x.shape[2], act_ref.shape[2])
     wide = 2 * half_w
     layers3, lanes3 = (cot_x.shape[0], cot_x.shape[2])
     inner3 = lanes3 - wide
-    layers2, lanes2 = (pre_x.shape[0], pre_x.shape[2])
-    own_layers, own_lanes = act_ref.shape[0], act_ref.shape[2]
+    layers2, lanes2 = (pre_x.shape[0], wide2.shape[2])
+    own_layers, own_rows = act_ref.shape[:2]
+    own_lanes = own_rows * wide
     rows2 = lanes2 // wide
     iota = lambda shape, dim: lax.broadcasted_iota(jnp.int32, shape, dim)
     depth, height = (me[1], me[2])
@@ -181,7 +201,7 @@
         perm2[t] = jnp.where(col2 == aim, 1.0, 0.0).astype(bf16)
     w3, w2 = (w3_ref[...].astype(bf16), w2_ref[...].astype(bf16))
     for t in range(9):
-        taps3[:, t * chan_three : (t + 1) * chan_three] = dot_t(perm3[t], w3).astype(bf16)
+        taps3[:, t * chan_three : (t + 1) * chan_three] = dot(perm3[t], w3).astype(bf16)
     for kd in range(3):
         taps2[kd * n2 : (kd + 1) * n2, :] = jnp.concatenate(
             [dot_t(perm2[kd * 3 + kw], w2) for kw in range(3)], axis=1
@@ -196,7 +216,7 @@
     coarse = own_layers // 2
     pool_wide[...] = jnp.zeros_like(pool_wide)
     for d in range(coarse):
-        total = leaky(pre_ref[2 * d].astype(f32)) + leaky(pre_ref[2 * d + 1].astype(f32))
+        total = leaky(in_rows(pre_ref, 2 * d)) + leaky(in_rows(pre_ref, 2 * d + 1))
         coarse_rows = inner3 // half_w
         sums = []
         for q in range(coarse_rows):
@@ -215,6 +235,22 @@
                     d + 2 - kd, kd * chan_two : (kd + 1) * chan_two, pair * wide : (pair + 1) * wide
                 ] = mean
 
+    def old_moment(layer, width):
+        pieces = [layer["moments"][c] for c in range(sizes[2])]
+        split = width // pieces[0].shape[1]
+        lines = [
+            pieces[c] if split == 1 else jnp.concatenate(pieces[c : c + split], axis=1)
+            for c in range(0, sizes[2], split)
+        ]
+        return lines[0] if len(lines) == 1 else jnp.concatenate(lines, axis=0)
+
+    finish(moment_copies)
+    decayed_copies = []
+    for layer in (layer2, layer3):
+        decayed = layer["decayed"].at[me[0], me[1]]
+        old = old_moment(layer, layer["decayed"].shape[3])
+        decayed[...] = (MOMENTUM * old).astype(bf16)
+        decayed_copies += send_all(lambda a, b: decayed, lambda n: decayed)
     finish_edges(0)
 
     back_acc[...] = jnp.zeros_like(back_acc)
@@ -260,39 +296,32 @@
             g3_acc[...] += ordered
 
     def first_sum(layer, acc):
-        parts = layer["parts"]
+        parts, arrived = (layer["parts"], layer["arrived"])
         rows = parts.shape[2]
         for i in range(sizes[0]):
             for j in range(sizes[1]):
                 at = (i * sizes[1] + j) * rows
                 parts[i, j] = acc[at : at + rows].astype(bf16)
-        return send(0, lambda other: parts.at[other], lambda j: layer["recv_a"].at[j])
+        return send_all(lambda a, b: parts.at[a, b], lambda n: arrived.at[n])
 
     def second_sum(layer, copies):
         finish(copies)
-        total = layer["parts"][me[0]].astype(f32)
-        for j in range(sizes[0] - 1):
-            total = total + layer["recv_a"][j].astype(f32)
-        layer["send_b"][...] = total.astype(bf16)
-        return send(
-            1, lambda other: layer["send_b"].at[other], lambda j: layer["recv_b"].at[j]
-        )
-
-    def third_sum(layer, copies):
+        total = layer["parts"][me[0], me[1]].astype(f32)
+        for n in range(len(peers)):
+            total = total + layer["arrived"][n].astype(f32)
+        layer["partial"][...] = total.astype(bf16)
+        layer["partials"][me[2]] = layer["partial"][...]
+        return send(2, lambda other: layer["partial"], lambda j: layer["partials"].at[me[2]])
+
+    def gather(layer, copies, rate, mom_ref):
         finish(copies)
-        total = layer["send_b"][me[1]].astype(f32)
-        for j in range(sizes[1] - 1):
-            total = total + layer["recv_b"][j].astype(f32)
-        layer["send_c"][...] = total.astype(bf16)
-        layer["recv_c"][me[2]] = layer["send_c"][...]
-        return send(2, lambda other: layer["send_c"], lambda j: layer["recv_c"].at[me[2]])
-
-    def summed(layer, copies, rate):
-        finish(copies)
-        total = layer["recv_c"][0].astype(f32)
+        total = layer["partials"][0].astype(f32)
         for j in range(1, sizes[2]):
-            total = total + layer["recv_c"][j].astype(f32)
-        return total * rate
+            total = total + layer["partials"][j].astype(f32)
+        mom_ref[...] = total * rate
+        mine = layer["full"].at[me[0], me[1]]
+        mine[...] = mom_ref[...].astype(bf16)
+        return send_all(lambda a, b: mine, lambda n: mine)
 
     copies3 = first_sum(layer3, g3_acc)
     finish_edges(1)
@@ -308,20 +337,12 @@
         cells = [parent[:, (r + 1) // 2 * wide : ((r + 1) // 2 + 1) * wide] for r in range(rows2)]
         spread = jnp.concatenate(cells, axis=1)
         inside = edge * jnp.where(f == 0, above, jnp.where(f == layers2 - 1, below, 1.0))
-        value = spread * 0.125 * slope_of(pre_x[f].astype(f32))
+        value = spread * 0.125 * slope_of(in_rows(pre_x, f))
         value = jnp.where(inside > 0, value, 0.0)
         before = jnp.where(column2 == 0, 0.0, pltpu.roll(value, 1, 1))
         after = jnp.where(column2 == wide - 1, 0.0, pltpu.roll(value, lanes2 - 1, 1))
         for kw, moved in enumerate((after, value, before)):
             wide2[f, kw * chan_two : (kw + 1) * chan_two, :] = moved.astype(bf16)
-        product = dot(taps2[...], wide2[f])
-        for kd in range(3):
-            total = None
-            for kh in range(3):
-                at, start = ((kd * 3 + kh) * chan_one, (2 - kh) * wide)
-                term = product[at : at + chan_one, start : start + own_lanes]
-                total = term if total is None else total + term
-            into[f + kd] += total
 
     copies3 = second_sum(layer3, copies3)
 
@@ -329,7 +350,9 @@
     for d in range(own_layers):
         for kh in range(3):
             start = (2 - kh) * wide
-            act_wide[d, kh * chan_one : (kh + 1) * chan_one, start : start + own_lanes] = act_ref[d]
+            for r in range(own_rows):
+                at = start + r * wide
+                act_wide[d, kh * chan_one : (kh + 1) * chan_one, at : at + wide] = act_ref[d, r]
     n_wide = 3 * chan_two
     for kd in range(3):
         grad = dot_t(wide2[2 - kd], act_wide[0])
@@ -344,68 +367,49 @@
                 g2_acc[...] += ordered
 
     copies2 = first_sum(layer2, g2_acc)
-    copies3 = third_sum(layer3, copies3)
+    full3 = gather(layer3, copies3, rates[1], mom3_ref)
+
+    def input_step(f):
+        product = dot(taps2[...], wide2[f])
+        for kd in range(3):
+            total = None
+            for kh in range(3):
+                at, start = ((kd * 3 + kh) * chan_one, (2 - kh) * wide)
+                term = product[at : at + chan_one, start : start + own_lanes]
+                total = term if total is None else total + term
+            into[f + kd] += total
+
+    third = layers2 // 3
+    for f in range(third):
+        input_step(f)
+    copies2 = second_sum(layer2, copies2)
+    for f in range(third, 2 * third):
+        input_step(f)
+    full2 = gather(layer2, copies2, rates[0], mom2_ref)
+    for f in range(2 * third, layers2):
+        input_step(f)
     for d in range(own_layers):
-        gin_ref[d] = (scales[0] * into[d + 2]).astype(bf16)
-    finish(moment_copies)
-    copies2 = second_sum(layer2, copies2)
-    grad_three = summed(layer3, copies3, rates[1])
-    copies2 = third_sum(layer2, copies2)
-    grad_two = summed(layer2, copies2, rates[0])
-
-    squares = [
-        jnp.sum(jnp.sum(g * g, axis=0, keepdims=True), axis=1, keepdims=True)
-        for g in (grad_two, grad_three)
-    ]
-    line = lax.broadcasted_iota(jnp.int32, (8, 128), 0)
-    slot = me[0] * sizes[1] + me[1]
-    squared[slot] = jnp.where(line == 0, squares[0], squares[1])
-    copies = []
-    for i in range(sizes[0]):
-        for j in range(sizes[1]):
-            if i or j:
-                a, b = (lax.rem(me[0] + i, sizes[0]), lax.rem(me[1] + j, sizes[1]))
-                copy = remote(squared.at[slot], squared.at[slot], (a, b, me[2]))
-                copy.start()
-                copies.append(copy)
-    finish(copies)
-    total = squared[0]
-    for n in range(1, sizes[0] * sizes[1]):
-        total = total + squared[n]
-    norm_g = jnp.sqrt(total)
-    copies = []
-    layers = ((layer2, grad_two, mom2_ref), (layer3, grad_three, mom3_ref))
-    for n, (layer, grad, mom_ref) in enumerate(layers):
-        trust = TRUST * norms[n] / (norm_g[n : n + 1, 0:1] + EPSILON)
-        pieces = [layer["moments"][c] for c in range(sizes[2])]
-        split = grad.shape[1] // pieces[0].shape[1]
-        lines = [
-            pieces[c] if split == 1 else jnp.concatenate(pieces[c : c + split], axis=1)
-            for c in range(0, sizes[2], split)
-        ]
-        old = lines[0] if len(lines) == 1 else jnp.concatenate(lines, axis=0)
-        moment = MOMENTUM * old + LEARN * trust * grad
-        mom_ref[...] = moment
-        full = layer["full"]
-        full[me[0], me[1]] = moment.astype(bf16)
-        copies.append(send(
-            1, lambda other: full.at[me[0], me[1]], lambda j: full.at[me[0], me[1]]
-        ))
-
-    again = []
-    for (layer, _, _), sent in zip(layers, copies):
-        full = layer["full"]
-        finish(sent)
-        again.append(send(0, lambda other: full.at[me[0]], lambda j: full.at[me[0]]))
-    targets = ((w2_ref, new2_ref), (w3_ref, new3_ref))
-    for (layer, _, _), sent, (w_ref, new_ref) in zip(layers, again, targets):
-        full = layer["full"]
-        finish(sent)
-        rows = full.shape[2]
-        for i in range(sizes[0]):
-            for j in range(sizes[1]):
-                at = (i * sizes[1] + j) * rows
-                new_ref[at : at + rows, :] = w_ref[at : at + rows, :] - full[i, j].astype(f32)
+        value = (scales[0] * into[d + 2]).astype(bf16)
+        for r in range(own_rows):
+            gin_ref[d, r] = value[:, r * wide : (r + 1) * wide]
+
+    finish(decayed_copies)
+    steps = []
+    for n, (layer, copies, mom_ref) in enumerate(((layer2, full2, mom2_ref), (layer3, full3, mom3_ref))):
+        finish(copies)
+        full, decayed = (layer["full"], layer["decayed"])
+        blocks = [(i, j) for i in range(sizes[0]) for j in range(sizes[1])]
+        grad = jnp.concatenate([full[i, j].astype(f32) for i, j in blocks], axis=0)
+        square = jnp.sum(jnp.sum(grad * grad, axis=0, keepdims=True), axis=1, keepdims=True)
+        rate = LEARN * TRUST * norms[n] / (jnp.sqrt(square) + EPSILON)
+        mom_ref[...] = MOMENTUM * old_moment(layer, mom_ref.shape[1]) + rate * mom_ref[...]
+        held = jnp.concatenate([decayed[i, j].astype(f32) for i, j in blocks], axis=0)
+        steps.append(held + rate * grad)
+    new2_ref[...] = w2_ref[...] - steps[0]
+    width = steps[1].shape[1]
+    for at in range(0, width, 128):
+        end = min(at + 128, width)
+        new3_ref[at:end, :] = w3_ref[at:end, :] - steps[1][:, at:end].T
 
 
 def local(act_one, pre_two, cot_three, weight_two, weight_three, moment_two, moment_three):
@@ -420,9 +424,13 @@
     def by_layer(x):
         return x[0].reshape(x.shape[1], x.shape[2], -1).transpose(1, 0, 2)
 
-    act, cot, pre = (by_layer(act_one), by_layer(cot_three), by_layer(pre_two))
+    def by_row(x):
+        rows = x[0].reshape(x.shape[1], -1, x.shape[4]).transpose(1, 0, 2)
+        return rows.reshape(x.shape[2], x.shape[3], x.shape[1], x.shape[4])
+
+    act, cot, pre = (by_row(act_one), by_layer(cot_three), by_row(pre_two))
     layers3, lanes3 = (cot.shape[0] + 4, cot.shape[2] + 4 * half_w)
-    layers2, lanes2 = (pre.shape[0] + 2, pre.shape[2] + 2 * local_w)
+    layers2, lanes2 = (pre.shape[0] + 2, (pre.shape[1] + 2) * local_w)
     inner3 = lanes3 - 2 * half_w
     held, blocks, moments = ([], [], [])
     for weight, moment in ((weight_two, moment_two), (weight_three, moment_three)):
@@ -432,15 +440,14 @@
         blocks.append(jax.ShapeDtypeStruct((rows, width), f32))
         held += [
             pltpu.VMEM((sizes[0], sizes[1], rows, width), bf16),
-            pltpu.VMEM((sizes[0] - 1, sizes[1], rows, width), bf16),
-            pltpu.VMEM((sizes[1], rows, width), bf16),
-            pltpu.VMEM((sizes[1] - 1, rows, width), bf16),
+            pltpu.VMEM((sizes[0] * sizes[1] - 1, rows, width), bf16),
             pltpu.VMEM((rows, width), bf16),
             pltpu.VMEM((sizes[2], rows, width), bf16),
             pltpu.VMEM((sizes[2],) + moments[-1].shape, f32),
             pltpu.VMEM((sizes[0], sizes[1], rows, width), bf16),
+            pltpu.VMEM((sizes[0], sizes[1], rows, width), bf16),
         ]
-    copies = 16 + 4 * (sum(sizes) - 3) + 2 * (sizes[2] - 1) + sizes[0] * sizes[1] - 1
+    copies = 16 + 4 * (sizes[2] - 1) + 6 * (sizes[0] * sizes[1] - 1)
     vmem = pl.BlockSpec(memory_space=pltpu.VMEM)
     grad_input, new_weight_two, new_weight_three, block_two, block_three = pl.pallas_call(
         functools.partial(
@@ -450,14 +457,14 @@
         out_shape=(
             jax.ShapeDtypeStruct(act.shape, bf16),
             jax.ShapeDtypeStruct(weight_two.shape, f32),
-            jax.ShapeDtypeStruct(weight_three.shape, f32),
+            jax.ShapeDtypeStruct(weight_three.shape[::-1], f32),
             *blocks,
         ),
         in_specs=[vmem] * 7,
         out_specs=(vmem,) * 5,
         scratch_shapes=[
             pltpu.VMEM((layers3, chan_three, lanes3), bf16),
-            pltpu.VMEM((layers2, chan_two, lanes2), bf16),
+            pltpu.VMEM((layers2, lanes2 // local_w, chan_two, local_w), bf16),
             pltpu.VMEM((9, 3 * chan_two, 27 * chan_two), bf16),
             pltpu.VMEM((9, 3 * chan_one, 27 * chan_one), bf16),
             pltpu.VMEM((layers3, 9 * chan_three, inner3), bf16),
@@ -468,10 +475,9 @@
             pltpu.VMEM((layers3 - 2, chan_two, 2 * inner3), f32),
             pltpu.VMEM((local_d, 3 * chan_one, lanes2), bf16),
             pltpu.VMEM((local_d // 2 + 2, 3 * chan_two, inner3), bf16),
-            pltpu.VMEM((layers2 + 2, chan_one, act.shape[2]), f32),
+            pltpu.VMEM((layers2 + 2, chan_one, local_h * local_w), f32),
             pltpu.VMEM(weight_two.shape, f32),
             pltpu.VMEM(weight_three.shape, f32),
-            pltpu.VMEM((sizes[0] * sizes[1], 8, 128), f32),
             *held,
             pltpu.SemaphoreType.DMA((copies,)),
             pltpu.SemaphoreType.DMA((copies,)),
@@ -481,8 +487,9 @@
             collective_id=0, has_side_effects=True, vmem_limit_bytes=56 * 2**20
         ),
         name="step",
-    )(cot, pre, act, weight_two, weight_three, *moments)
-    grad_input = grad_input.transpose(1, 0, 2).reshape(act_one.shape)
+    )(cot, pre, act, weight_two, weight_three.T, *moments)
+    grad_input = grad_input.transpose(2, 0, 1, 3)[None]
+    new_weight_three = new_weight_three.T
     mine = lax.axis_index("height")
     new_moment_two, new_moment_three = (
         lax.dynamic_slice_in_dim(block.reshape(-1), mine * moment.shape[0], moment.shape[0])

time: 84.1 us -> 70.7 us (0.84)
  Pallas kernels: 68.4 us -> 57.3 us
  local copies, waits for them, and re-layouts: 14 us -> 12.4 us
    pallas_call x1, Pallas kernels: 68.4 us -> 57.3 us  [local(): pl.pallas_call(functools.partial(step_kernel, half_w, (scale_two, scale_t...]
    unnamed x22 -> x18, local copies, waits for them, and re-layouts: 6.99 us -> 5.43 us
    another operation x4 -> x2, local copies, waits for them, and re-layouts: 4.09 us -> 4.06 us  [by_row(): rows = x[0].reshape(x.shape[1], -1, x.shape[4]).transpose(1, 0, 2)]
where the time goes in v2:
time: 70.7 us; the launch traced here: 70.4 us
  Pallas kernels  57.3 us (81%)
  local copies, waits for them, and re-layouts  12.4 us (18%)
    pallas_call x1, Pallas kernels, local(): pl.pallas_call(functools.partial(step_kernel, half_w, (scale_two, scale_t...  57.3 us
    unnamed x18, local copies, waits for them, and re-layouts  5.43 us
    another operation x2, local copies, waits for them, and re-layouts, by_row(): rows = x[0].reshape(x.shape[1], -1, x.shape[4]).transpose(1, 0, 2)  4.06 us

profile of v2, /device:TPU:0, one launch (start us, length us, event | category | flops | bytes accessed | tf_op | source)
XLA Modules:
  0.0 70.4 jit_solution(13524101855326580560)
XLA Ops:
  0.6 1.7 %copy.17 = bf16[1,128,2,512]{3,1,2,0:T(8,128)(2,1)} copy(bf16[1,128,2,512]{3,2,1,0:T(2,128)(2,1)} %param.9) | data formatting | bytes 524288 | tf_op args[2]
  2.3 0.0 copy-start.1
  2.3 2.9 %copy.13 = bf16[64,64,128]{2,0,1:T(8,128)(2,1)} copy(bf16[64,64,128]{2,1,0:T(8,128)(2,1)} %bitcast.21) | data formatting | bytes 2097152 | tf_op jit(solution)/shard_map/reshape;squeeze | solution.py:428
  5.2 0.0 copy-done.1
  5.2 1.1 %copy.14 = bf16[32,64,128]{2,0,1:T(8,128)(2,1)} copy(bf16[32,64,128]{2,1,0:T(8,128)(2,1)S(1)} %bitcast.24) | data formatting | bytes 1048576 | tf_op jit(solution)/shard_map/reshape;squeeze | solution.py:428
  6.4 0.0 copy-done.6
  6.4 0.7 reshape.30.m2_ref
  7.1 0.0 copy-done.4
  7.1 0.7 reshape.31.m3_ref
  7.8 57.3 %step.1 = (bf16[4,16,32,128]{3,2,1,0:T(8,128)(2,1)}, f32[64,864]{1,0:T(8,128)}, f32[1728,128]{1,0:T(8,128)}, f32[8,864]{1,0:T(8,128)}, f32[16,1728]{1,0:T(8,128)}) custom-call(bf16[2,128,512]{2,1,0:T(8,128)(2,1)} %bitcast.20, bf16[4,16,64,128]{3,2,1,0:T(8,128)(2,1)} %bitcast.18, bf16[4,16,32,128]{3,2,1,0:T(8,128)(2,1)} %bitcast.19, f32[64,864]{1,0:T(8,128)} %w2_ref.1, ...), custom_call_target="tpu_custom_call" | custom-call | tf_op jit(solution)/shard_map/step/pallas_call | solution.py:452
  65.1 0.0 copy-start.5
  65.1 0.0 copy-start.3
  65.1 0.0 copy-start
  65.1 2.1 %copy.15 = bf16[1,32,4,16,128]{4,3,2,1,0:T(8,128)(2,1)} copy(bf16[1,32,4,16,128]{4,1,3,2,0:T(8,128)(2,1)} %bitcast.25) | data formatting | bytes 1048576
  67.3 0.0 copy-done.5
  67.3 0.1 reshape.32
  67.3 0.7 dynamic_slice.6
  68.0 0.0 copy-done.3
  68.0 0.1 reshape.33
  68.1 0.7 dynamic_slice.7
  68.8 0.0 copy-done.2
  68.8 0.7 copy.20
  69.5 0.0 copy-done
  69.5 0.9 %copy.21 = f32[128,1728]{0,1:T(8,128)} copy(f32[128,1728]{0,1:T(8,128)S(1)} %bitcast.23) | data formatting | bytes 1769472
  (3 shorter events, 0.0 us)
Async XLA Ops:
  2.3 2.9 %copy-start.1 = (bf16[1,32,4,16,128]{4,3,2,1,0:T(8,128)(2,1)S(1)}, bf16[1,32,4,16,128]{4,3,2,1,0:T(8,128)(2,1)}, u32[]{:S(2)}) copy-start(bf16[1,32,4,16,128]{4,3,2,1,0:T(8,128)(2,1)} %param.7) | copy-start | bytes 1572868
  5.2 1.1 %copy-start.6 = (f32[1728]{0:T(1024)S(1)}, f32[1728]{0:T(1024)}, u32[]{:S(2)}) copy-start(f32[1728]{0:T(1024)} %param.12) | copy-start | bytes 20740
  5.2 1.8 %copy-start.4 = (f32[6912]{0:T(1024)S(1)}, f32[6912]{0:T(1024)}, u32[]{:S(2)}) copy-start(f32[6912]{0:T(1024)} %param.13) | copy-start | bytes 82948
  65.1 2.2 %copy-start.5 = (f32[8,864]{1,0:T(8,128)S(1)}, f32[8,864]{1,0:T(8,128)}, u32[]{:S(2)}) copy-start(f32[8,864]{1,0:T(8,128)} %get-tuple-element.13) | copy-start | bytes 82948
  65.1 2.9 %copy-start.3 = (f32[16,1728]{1,0:T(8,128)S(1)}, f32[16,1728]{1,0:T(8,128)}, u32[]{:S(2)}) copy-start(f32[16,1728]{1,0:T(8,128)} %get-tuple-element.14) | copy-start | bytes 331780
  65.1 4.4 %copy-start = (f32[1728,128]{1,0:T(8,128)S(1)}, f32[1728,128]{1,0:T(8,128)}, u32[]{:S(2)}) copy-start(f32[1728,128]{1,0:T(8,128)} %get-tuple-element.12) | copy-start | bytes 2654212
  67.3 1.6 %copy-start.2 = (f32[64,864]{1,0:T(8,128)S(1)}, f32[64,864]{1,0:T(8,128)}, u32[]{:S(2)}) copy-start(f32[64,864]{1,0:T(8,128)} %get-tuple-element.26) | copy-start | bytes 663556

commit v3 on v2

--- a/solution.py
+++ b/solution.py
@@ -139,10 +139,13 @@
             )
             edges[a].append((d, h, copy))
 
+    def start_edges(a):
+        for d, h, copy in edges[a]:
             @pl.when(present(d, h))
             def _():
                 copy.start()
 
+    start_edges(0)
     own = []
     for a, (ref, out, width) in enumerate(arrays):
         copy = pltpu.make_async_copy(ref, out.at[place(ref, width, 0, 0, False)], own_sem.at[a])
@@ -244,14 +247,8 @@
         ]
         return lines[0] if len(lines) == 1 else jnp.concatenate(lines, axis=0)
 
-    finish(moment_copies)
-    decayed_copies = []
-    for layer in (layer2, layer3):
-        decayed = layer["decayed"].at[me[0], me[1]]
-        old = old_moment(layer, layer["decayed"].shape[3])
-        decayed[...] = (MOMENTUM * old).astype(bf16)
-        decayed_copies += send_all(lambda a, b: decayed, lambda n: decayed)
     finish_edges(0)
+    start_edges(1)
 
     back_acc[...] = jnp.zeros_like(back_acc)
     column3 = iota((1, lanes3), 1) % half_w
@@ -345,6 +342,13 @@
             wide2[f, kw * chan_two : (kw + 1) * chan_two, :] = moved.astype(bf16)
 
     copies3 = second_sum(layer3, copies3)
+    finish(moment_copies)
+    decayed_copies = []
+    for layer in (layer2, layer3):
+        decayed = layer["decayed"].at[me[0], me[1]]
+        old = old_moment(layer, layer["decayed"].shape[3])
+        decayed[...] = (MOMENTUM * old).astype(bf16)
+        decayed_copies += send_all(lambda a, b: decayed, lambda n: decayed)
 
     act_wide[...] = jnp.zeros_like(act_wide)
     for d in range(own_layers):

time: 70.7 us -> 70.1 us (level)
  no operation moved by 1% of the time
where the time goes in v3:
time: 70.1 us; the launch traced here: 69.8 us
  Pallas kernels  56.8 us (81%)
  local copies, waits for them, and re-layouts  12.4 us (18%)
    pallas_call x1, Pallas kernels, local(): pl.pallas_call(functools.partial(step_kernel, half_w, (scale_two, scale_t...  56.8 us
    unnamed x18, local copies, waits for them, and re-layouts  5.43 us
    another operation x2, local copies, waits for them, and re-layouts, by_row(): rows = x[0].reshape(x.shape[1], -1, x.shape[4]).transpose(1, 0, 2)  4.06 us

profile of v3, /device:TPU:0, one launch (start us, length us, event | category | flops | bytes accessed | tf_op | source)
XLA Modules:
  0.0 69.8 jit_solution(17525938600321331219)
XLA Ops:
  0.6 1.7 %copy.17 = bf16[1,128,2,512]{3,1,2,0:T(8,128)(2,1)} copy(bf16[1,128,2,512]{3,2,1,0:T(2,128)(2,1)} %param.9) | data formatting | bytes 524288 | tf_op args[2]
  2.3 0.0 copy-start.1
  2.3 2.9 %copy.13 = bf16[64,64,128]{2,0,1:T(8,128)(2,1)} copy(bf16[64,64,128]{2,1,0:T(8,128)(2,1)} %bitcast.21) | data formatting | bytes 2097152 | tf_op jit(solution)/shard_map/reshape;squeeze | solution.py:432
  5.2 0.0 copy-done.1
  5.2 1.1 %copy.14 = bf16[32,64,128]{2,0,1:T(8,128)(2,1)} copy(bf16[32,64,128]{2,1,0:T(8,128)(2,1)S(1)} %bitcast.24) | data formatting | bytes 1048576 | tf_op jit(solution)/shard_map/reshape;squeeze | solution.py:432
  6.4 0.0 copy-done.6
  6.4 0.7 reshape.30.m2_ref
  7.1 0.0 copy-done.4
  7.1 0.7 reshape.31.m3_ref
  7.8 56.8 %step.1 = (bf16[4,16,32,128]{3,2,1,0:T(8,128)(2,1)}, f32[64,864]{1,0:T(8,128)}, f32[1728,128]{1,0:T(8,128)}, f32[8,864]{1,0:T(8,128)}, f32[16,1728]{1,0:T(8,128)}) custom-call(bf16[2,128,512]{2,1,0:T(8,128)(2,1)} %bitcast.20, bf16[4,16,64,128]{3,2,1,0:T(8,128)(2,1)} %bitcast.18, bf16[4,16,32,128]{3,2,1,0:T(8,128)(2,1)} %bitcast.19, f32[64,864]{1,0:T(8,128)} %w2_ref.1, ...), custom_call_target="tpu_custom_call" | custom-call | tf_op jit(solution)/shard_map/step/pallas_call | solution.py:456
  64.5 0.0 copy-start.5
  64.5 0.0 copy-start.3
  64.5 0.0 copy-start
  64.6 2.1 %copy.15 = bf16[1,32,4,16,128]{4,3,2,1,0:T(8,128)(2,1)} copy(bf16[1,32,4,16,128]{4,1,3,2,0:T(8,128)(2,1)} %bitcast.25) | data formatting | bytes 1048576
  66.7 0.0 copy-done.5
  66.7 0.1 reshape.32
  66.8 0.7 dynamic_slice.6
  67.4 0.0 copy-done.3
  67.4 0.1 reshape.33
  67.5 0.7 dynamic_slice.7
  68.2 0.0 copy-done.2
  68.2 0.7 copy.20
  68.9 0.0 copy-done
  68.9 0.9 %copy.21 = f32[128,1728]{0,1:T(8,128)} copy(f32[128,1728]{0,1:T(8,128)S(1)} %bitcast.23) | data formatting | bytes 1769472
  (3 shorter events, 0.0 us)
Async XLA Ops:
  2.3 2.9 %copy-start.1 = (bf16[1,32,4,16,128]{4,3,2,1,0:T(8,128)(2,1)S(1)}, bf16[1,32,4,16,128]{4,3,2,1,0:T(8,128)(2,1)}, u32[]{:S(2)}) copy-start(bf16[1,32,4,16,128]{4,3,2,1,0:T(8,128)(2,1)} %param.7) | copy-start | bytes 1572868
  5.2 1.1 %copy-start.6 = (f32[1728]{0:T(1024)S(1)}, f32[1728]{0:T(1024)}, u32[]{:S(2)}) copy-start(f32[1728]{0:T(1024)} %param.12) | copy-start | bytes 20740
  5.2 1.8 %copy-start.4 = (f32[6912]{0:T(1024)S(1)}, f32[6912]{0:T(1024)}, u32[]{:S(2)}) copy-start(f32[6912]{0:T(1024)} %param.13) | copy-start | bytes 82948
  64.5 2.2 %copy-start.5 = (f32[8,864]{1,0:T(8,128)S(1)}, f32[8,864]{1,0:T(8,128)}, u32[]{:S(2)}) copy-start(f32[8,864]{1,0:T(8,128)} %get-tuple-element.13) | copy-start | bytes 82948
  64.5 2.9 %copy-start.3 = (f32[16,1728]{1,0:T(8,128)S(1)}, f32[16,1728]{1,0:T(8,128)}, u32[]{:S(2)}) copy-start(f32[16,1728]{1,0:T(8,128)} %get-tuple-element.14) | copy-start | bytes 331780
  64.5 4.4 %copy-start = (f32[1728,128]{1,0:T(8,128)S(1)}, f32[1728,128]{1,0:T(8,128)}, u32[]{:S(2)}) copy-start(f32[1728,128]{1,0:T(8,128)} %get-tuple-element.12) | copy-start | bytes 2654212
  66.7 1.6 %copy-start.2 = (f32[64,864]{1,0:T(8,128)S(1)}, f32[64,864]{1,0:T(8,128)}, u32[]{:S(2)}) copy-start(f32[64,864]{1,0:T(8,128)} %get-tuple-element.26) | copy-start | bytes 663556
